TPU v7x, 32 devices: a whole 2x2x4 slice. The times are simulated.
32 devices in a mesh: groups: 2 (over y), expert: 8 (over z, x), dp: 2 (over core).
Axes of the slice: x: 2, y: 2, z: 4, core: 2. Of those that a mesh axis runs over, the one named last changes fastest.
Arguments:
- tokens: bfloat16 [4096, 2880], P(('groups', 'expert', 'dp')), parts along dimension 0, may hold values from -6 to 6
- cotangent: bfloat16 [4096, 2880], P(('groups', 'expert', 'dp')), parts along dimension 0, may hold values from -1.5 to 1.5
- expert_ids: int32 [4096, 4], P(('groups', 'expert', 'dp')), parts along dimension 0, may hold values from 0 to 127, as said below
- route_weight: float32 [4096, 4], P(('groups', 'expert', 'dp')), parts along dimension 0, may hold values from 0.1 to 1
- gate_weight: bfloat16 [20480, 2880], P(('expert', 'dp')), may hold values from -0.109375 to 0.109375
- up_weight: bfloat16 [20480, 2880], P(('expert', 'dp')), may hold values from -0.109375 to 0.109375
- down_weight: bfloat16 [20480, 2880], P(('expert', 'dp')), may hold values from -0.125 to 0.125
Outputs:
- grad_tokens: bfloat16 [4096, 2880], P(('groups', 'expert', 'dp')), parts along dimension 0
- grad_gate: bfloat16 [40960, 2880], P(('groups', 'expert', 'dp')), parts along dimension 0
- grad_up: bfloat16 [40960, 2880], P(('groups', 'expert', 'dp')), parts along dimension 0
- grad_down: bfloat16 [40960, 2880], P(('groups', 'expert', 'dp')), parts along dimension 0
There are 2 independent parts, one for each index of `groups`. A program takes and returns all parts, laid end to end along the dimension named above; an argument that names none is the same for every part. Nothing has to cross between parts.
Inputs may be any that keep to these rules, and one draw needn't show every extreme that they name: `expert_ids`: the 4 ids of a token are distinct and differ modulo 4. In each aligned block of 128 tokens (the tokens of one device) each expert below 8 is named at least once and at most 4 times; one of them, the same in every block, is named exactly 4 times in every block.
All inputs are finite; a program needn't handle non-finite values.
Results may differ from a plain program's by a relative error of at most 0.0066.
Values may be sent and summed in bfloat16 or wider, within the bound.
A program may use at most 256 MiB of HBM per device.

v0:
```python
import jax
import jax.numpy as jnp
from jax import lax
from jax.sharding import PartitionSpec as P

E_WIN = 8
CAP = 4


def expert_backward(rows_x, rows_c, w_gate, w_up, w_down):
    contract_last = (((1,), (1,)), ((), ()))
    gate_pre = lax.dot_general(rows_x, w_gate, contract_last, preferred_element_type=jnp.float32)
    up_pre = lax.dot_general(rows_x, w_up, contract_last, preferred_element_type=jnp.float32)
    d_act = lax.dot_general(rows_c, w_down, contract_last, preferred_element_type=jnp.float32)
    sigmoid_gate = jax.nn.sigmoid(1.702 * gate_pre)
    gated = gate_pre * sigmoid_gate
    activation = ((up_pre + 1.0) * gated).astype(jnp.bfloat16)
    d_up = (d_act * gated).astype(jnp.bfloat16)
    d_gate = (
        d_act
        * (up_pre + 1.0)
        * (sigmoid_gate + 1.702 * gate_pre * sigmoid_gate * (1.0 - sigmoid_gate))
    ).astype(jnp.bfloat16)
    partial_value = jnp.dot(d_gate, w_gate, preferred_element_type=jnp.float32) + jnp.dot(
        d_up, w_up, preferred_element_type=jnp.float32
    )
    return (activation, d_gate, d_up, partial_value)


def weight_terms(rows_x, rows_c, activation, d_gate, d_up):
    contract_first = (((0,), (0,)), ((), ()))
    term_gate = lax.dot_general(
        d_gate, rows_x, contract_first, preferred_element_type=jnp.float32
    ).astype(jnp.bfloat16)
    term_up = lax.dot_general(
        d_up, rows_x, contract_first, preferred_element_type=jnp.float32
    ).astype(jnp.bfloat16)
    term_down = lax.dot_general(
        activation, rows_c, contract_first, preferred_element_type=jnp.float32
    ).astype(jnp.bfloat16)
    return lax.optimization_barrier((term_gate, term_up, term_down))


def body(tokens, cotangent, expert_ids, route_weight, gate_weight, up_weight, down_weight):
    devices = lax.axis_size("expert")
    group_size = devices // E_WIN
    model_width = tokens.shape[1]
    window_ids = jnp.arange(E_WIN, dtype=jnp.int32)
    matches = expert_ids[:, :, None] == window_ids[None, None, :]
    member = jnp.any(matches, axis=1)
    weight_of = jnp.sum(jnp.where(matches, route_weight[:, :, None], 0.0), axis=1)
    position = jnp.cumsum(member.astype(jnp.int32), axis=0) - 1
    slot_ids = jnp.arange(CAP, dtype=jnp.int32)
    placement = jnp.logical_and(
        member.T[:, None, :], position.T[:, None, :] == slot_ids[None, :, None]
    )
    place_half = placement.astype(jnp.bfloat16)
    place_full = placement.astype(jnp.float32)
    picked_x = jnp.einsum(
        "kct,td->kcd", place_half, tokens, preferred_element_type=jnp.float32
    ).astype(jnp.bfloat16)
    picked_dy = jnp.einsum("kct,td->kcd", place_half, cotangent, preferred_element_type=jnp.float32)
    slot_weight = jnp.einsum("kct,tk->kc", place_full, weight_of, precision=lax.Precision.HIGHEST)
    picked_c = (slot_weight[:, :, None] * picked_dy).astype(jnp.bfloat16)
    send_x = jnp.repeat(picked_x, group_size, axis=0)
    send_c = jnp.repeat(picked_c, group_size, axis=0)
    recv_x, recv_c = (
        lax.all_to_all(send_x, "expert", split_axis=0, concat_axis=0, tiled=True),
        lax.all_to_all(send_c, "expert", split_axis=0, concat_axis=0, tiled=True),
    )
    rows_x = recv_x.reshape(devices * CAP, model_width)
    rows_c = recv_c.reshape(devices * CAP, model_width)
    full_gate, full_up, full_down = (
        lax.all_gather(gate_weight, "dp", axis=0, tiled=True),
        lax.all_gather(up_weight, "dp", axis=0, tiled=True),
        lax.all_gather(down_weight, "dp", axis=0, tiled=True),
    )
    activation, d_gate, d_up, partial_value = expert_backward(
        rows_x, rows_c, full_gate, full_up, full_down
    )
    part_rows = partial_value.astype(jnp.bfloat16)
    term_gate, term_up, term_down = weight_terms(rows_x, rows_c, activation, d_gate, d_up)
    summed = (
        lax.psum_scatter(
            term_gate.astype(jnp.float32).astype(jnp.bfloat16),
            "dp",
            scatter_dimension=0,
            tiled=True,
        ).astype(jnp.float32),
        lax.psum_scatter(
            term_up.astype(jnp.float32).astype(jnp.bfloat16), "dp", scatter_dimension=0, tiled=True
        ).astype(jnp.float32),
        lax.psum_scatter(
            term_down.astype(jnp.float32).astype(jnp.bfloat16),
            "dp",
            scatter_dimension=0,
            tiled=True,
        ).astype(jnp.float32),
    )
    grad_gate = summed[0].astype(jnp.bfloat16)
    grad_up = summed[1].astype(jnp.bfloat16)
    grad_down = summed[2].astype(jnp.bfloat16)
    returned = lax.all_to_all(
        part_rows.reshape(devices, CAP, model_width),
        "expert",
        split_axis=0,
        concat_axis=0,
        tiled=True,
    )
    combined = jnp.sum(
        returned.astype(jnp.float32).reshape(E_WIN, group_size, CAP, model_width), axis=1
    )
    grad_tokens = jnp.einsum(
        "kct,kcd->td", place_full, combined, precision=lax.Precision.HIGHEST
    ).astype(jnp.bfloat16)
    return (grad_tokens, grad_gate, grad_up, grad_down)


def solution(mesh):
    return jax.shard_map(
        body,
        mesh=mesh,
        in_specs=(
            P(("groups", "expert", "dp"), None),
            P(("groups", "expert", "dp"), None),
            P(("groups", "expert", "dp"), None),
            P(("groups", "expert", "dp"), None),
            P(("expert", "dp"), None),
            P(("expert", "dp"), None),
            P(("expert", "dp"), None),
        ),
        out_specs=(
            P(("groups", "expert", "dp"), None),
            P(("groups", "expert", "dp"), None),
            P(("groups", "expert", "dp"), None),
            P(("groups", "expert", "dp"), None),
        ),
        check_vma=False,
    )
```

profile of v0, /device:TPU:0, one launch (start us, length us, event | category | flops | bytes accessed | tf_op | source)
XLA Modules:
  0.0 210.2 jit_solution(11081123148681055565)
XLA Ops:
  7.2 0.0 copy-start
  7.2 0.0 copy-start.3
  7.2 0.0 copy-start.4
  7.2 0.0 copy-start.2
  7.2 0.0 all-gather.8.cloned.1.call-start
  7.3 0.7 all-gather.8.cloned.1.call-update
  7.9 0.0 all-gather.6.cloned.1.call-start
  8.0 0.7 all-gather.6.cloned.1.call-update
  8.7 0.0 all-gather.4.cloned.1.call-start
  8.7 0.7 all-gather.4.cloned.1.call-update
  9.4 0.0 copy-done.3
  9.5 0.1 copy.30
  9.6 0.2 reduce_window_sum.11
  9.8 0.0 copy-done.4
  9.8 0.2 fusion.10
  10.0 0.1 copy.37
  10.1 0.0 copy-done
  10.1 0.4 fusion.1
  10.4 0.8 copy.32
  11.2 7.3 %all-to-all-start = ((bf16[8,4,2880]{2,1,0:T(4,128)(2,1)}), bf16[8,4,2880]{2,1,0:T(4,128)(2,1)S(1)}, u32[]{:S(2)}, u32[]{:S(2)}) async-start(bf16[8,4,2880]{2,1,0:T(4,128)(2,1)} %copy.32), calls=%async_computation | async-start | bytes 376832 | tf_op jit(solution)/shard_map/all_to_all | solution.py:69
  18.5 0.0 copy-done.2
  18.5 0.4 convolution_convert_fusion.3
  18.8 0.8 copy.33
  19.6 6.7 %all-to-all-done = bf16[8,4,2880]{2,1,0:T(4,128)(2,1)S(1)} async-done(((bf16[8,4,2880]{2,1,0:T(4,128)(2,1)}), bf16[8,4,2880]{2,1,0:T(4,128)(2,1)S(1)}, u32[]{:S(2)}, u32[]{:S(2)}) %all-to-all-start) | async-done | bytes 184352 | tf_op jit(solution)/shard_map/all_to_all | solution.py:69
  26.3 3.4 %all-to-all-start.1 = ((bf16[8,4,2880]{2,1,0:T(4,128)(2,1)}), bf16[8,4,2880]{2,1,0:T(4,128)(2,1)S(1)}, u32[]{:S(2)}, u32[]{:S(2)}) async-start(bf16[8,4,2880]{2,1,0:T(4,128)(2,1)} %copy.33), calls=%async_computation.1 | async-start | bytes 376832 | tf_op jit(solution)/shard_map/all_to_all | solution.py:68
  29.7 0.0 reduce-scatter.4.cloned.1.call-start
  29.7 0.1 reshape.25
  29.8 7.5 %all-to-all-done.1 = bf16[8,4,2880]{2,1,0:T(4,128)(2,1)S(1)} async-done(((bf16[8,4,2880]{2,1,0:T(4,128)(2,1)}), bf16[8,4,2880]{2,1,0:T(4,128)(2,1)S(1)}, u32[]{:S(2)}, u32[]{:S(2)}) %all-to-all-start.1) | async-done | bytes 184352 | tf_op jit(solution)/shard_map/all_to_all | solution.py:68
  37.4 0.1 reshape.26
  37.4 2.0 all-gather.8.cloned.1.call-done
  39.4 7.8 %fusion.14 = f32[32,2560]{1,0:T(8,128)S(1)} fusion(bf16[32,2880]{1,0:T(8,128)(2,1)S(1)} %reshape.26, bf16[2560,2880]{0,1:T(8,128)(2,1)} %all-gather.8.cloned.1.call-done), kind=kOutput, calls=%fused_computation.29 | convolution fusion | flops 471859200 | bytes 15257600 | tf_op jit(solution)/shard_map/dot_general | solution.py:12
  47.2 22.1 %all-gather.6.cloned.1.call-done = bf16[2560,2880]{0,1:T(8,128)(2,1)} async-done(((bf16[1280,2880]{0,1:T(8,128)(2,1)}), bf16[2560,2880]{0,1:T(8,128)(2,1)}) %all-gather.6.cloned.1.call-update) | async-done | bytes 14745616 | tf_op jit(solution)/shard_map/all_gather | solution.py:75
  69.3 7.8 %convolution_add_fusion = f32[32,2560]{1,0:T(8,128)S(1)} fusion(bf16[32,2880]{1,0:T(8,128)(2,1)S(1)} %reshape.26, bf16[2560,2880]{0,1:T(8,128)(2,1)} %all-gather.6.cloned.1.call-done), kind=kOutput, calls=%fused_computation.5 | convolution fusion | flops 471941120 | bytes 15257600 | tf_op jit(solution)/shard_map/dot_general | solution.py:13
  77.1 10.8 %convolution_convert_fusion = bf16[2560,2880]{0,1:T(8,128)(2,1)} fusion(bf16[32,2880]{1,0:T(8,128)(2,1)S(1)} %reshape.25, f32[32,2560]{1,0:T(8,128)S(1)} %convolution_add_fusion, f32[32,2560]{1,0:T(8,128)S(1)} %fusion.14), kind=kOutput, calls=%fused_computation | convolution fusion | flops 479805440 | bytes 15585280 | tf_op jit(solution)/shard_map/dot_general | solution.py:38
  87.9 11.4 %all-gather.4.cloned.1.call-done = bf16[2560,2880]{0,1:T(8,128)(2,1)} async-done(((bf16[1280,2880]{0,1:T(8,128)(2,1)}), bf16[2560,2880]{0,1:T(8,128)(2,1)}) %all-gather.4.cloned.1.call-update) | async-done | bytes 14745616 | tf_op jit(solution)/shard_map/all_gather | solution.py:76
  99.3 7.8 %multiply_convert_fusion.1 = (bf16[32,2560]{1,0:T(8,128)(2,1)S(1)}, bf16[32,2560]{1,0:T(8,128)(2,1)S(1)}) fusion(f32[32,2560]{1,0:T(8,128)S(1)} %fusion.14, f32[32,2560]{1,0:T(8,128)S(1)} %convolution_add_fusion, bf16[32,2880]{1,0:T(8,128)(2,1)S(1)} %reshape.25, bf16[2560,2880]{0,1:T(8,128)(2,1)} %all-gather.4.cloned.1.call-done), kind=kOutput, calls=%fused_computation.14 | convolution fusion | flops 473006080 | bytes 15912960 | tf_op jit(solution)/shard_map/dot_general | solution.py:14
  107.2 7.4 %convolution_convert_fusion.1 = bf16[2560,2880]{0,1:T(8,128)(2,1)} fusion(bf16[32,2560]{1,0:T(8,128)(2,1)S(1)} %get-tuple-element.10, bf16[32,2880]{1,0:T(8,128)(2,1)S(1)} %reshape.26), kind=kOutput, calls=%fused_computation.1 | convolution fusion | flops 479232000 | bytes 15093760 | tf_op jit(solution)/shard_map/dot_general | solution.py:35
  114.5 7.4 %convolution_convert_fusion.2 = bf16[2560,2880]{0,1:T(8,128)(2,1)} fusion(bf16[32,2560]{1,0:T(8,128)(2,1)S(1)} %get-tuple-element.11, bf16[32,2880]{1,0:T(8,128)(2,1)S(1)} %reshape.26), kind=kOutput, calls=%fused_computation.2 | convolution fusion | flops 479232000 | bytes 15093760 | tf_op jit(solution)/shard_map/dot_general | solution.py:32
  122.0 0.0 reduce-scatter.4.cloned.1.call-update
  122.0 0.0 reduce-scatter.6.cloned.1.call-start
  122.0 0.5 reduce-scatter.6.cloned.1.call-update
  122.6 0.2 reduce-scatter.8.cloned.1.call-start
  122.8 0.3 reduce-scatter.8.cloned.1.call-update
  123.2 0.0 copy-start.1
  123.2 9.6 %fusion.15 = f32[32,2880]{1,0:T(8,128)S(1)} fusion(bf16[32,2560]{1,0:T(8,128)(2,1)S(1)} %get-tuple-element.11, bf16[2560,2880]{0,1:T(8,128)(2,1)} %all-gather.8.cloned.1.call-done), kind=kOutput, calls=%fused_computation.30 | convolution fusion | flops 471859200 | bytes 15278080 | tf_op jit(solution)/shard_map/dot_general | solution.py:24
  132.8 13.0 %fusion.2 = bf16[32,2880]{1,0:T(8,128)(2,1)S(1)} fusion(f32[32,2880]{1,0:T(8,128)S(1)} %fusion.15, bf16[32,2560]{1,0:T(8,128)(2,1)S(1)} %get-tuple-element.10, bf16[2560,2880]{0,1:T(8,128)(2,1)} %all-gather.6.cloned.1.call-done), kind=kOutput, calls=%fused_computation.10 | convolution fusion | flops 472043520 | bytes 15462400 | tf_op jit(solution)/shard_map/dot_general | solution.py:24
  145.8 0.1 reshape.27
  145.9 13.9 %all_to_all.15 = bf16[8,4,2880]{2,1,0:T(4,128)(2,1)S(1)} all-to-all(bf16[8,4,2880]{2,1,0:T(4,128)(2,1)S(1)} %reshape.27), channel_id=1, replica_groups=mesh['groups'=2,'expert'=8,'dp'=2] {'expert'}, dimensions={0} | all-to-all | bytes 368640 | tf_op jit(solution)/shard_map/all_to_all | solution.py:103
  159.8 1.3 fusion
  161.0 0.0 reduce-scatter.4.cloned.1.call-done
  161.0 14.4 %reduce-scatter.6.cloned.1.call-done = bf16[1280,2880]{0,1:T(8,128)(2,1)} async-done(((bf16[2560,2880]{0,1:T(8,128)(2,1)}), bf16[1280,2880]{0,1:T(8,128)(2,1)}) %reduce-scatter.6.cloned.1.call-update) | async-done | bytes 7372816 | tf_op jit(solution)/shard_map/reduce_scatter | solution.py:90
  175.4 27.9 %reduce-scatter.8.cloned.1.call-done = bf16[1280,2880]{0,1:T(8,128)(2,1)} async-done(((bf16[2560,2880]{0,1:T(8,128)(2,1)}), bf16[1280,2880]{0,1:T(8,128)(2,1)}) %reduce-scatter.8.cloned.1.call-update) | async-done | bytes 7372816 | tf_op jit(solution)/shard_map/reduce_scatter | solution.py:93
  203.3 0.0 copy-done.1
  (6 shorter events, 0.1 us)
Async XLA Ops:
  7.2 2.9 %copy-start = (bf16[128,2880]{0,1:T(8,128)(2,1)S(1)}, bf16[128,2880]{0,1:T(8,128)(2,1)}, u32[]{:S(2)}) copy-start(bf16[128,2880]{0,1:T(8,128)(2,1)} %param.8) | copy-start | bytes 2211844
  7.2 2.3 %copy-start.3 = (s32[128,4]{0,1:T(4,128)S(1)}, s32[128,4]{0,1:T(4,128)}, u32[]{:S(2)}) copy-start(s32[128,4]{0,1:T(4,128)} %param.9) | copy-start | bytes 6148
  7.2 2.6 %copy-start.4 = (f32[128,4]{0,1:T(4,128)S(1)}, f32[128,4]{0,1:T(4,128)}, u32[]{:S(2)}) copy-start(f32[128,4]{0,1:T(4,128)} %param.10) | copy-start | bytes 6148
  7.2 11.3 %copy-start.2 = (bf16[128,2880]{0,1:T(8,128)(2,1)S(1)}, bf16[128,2880]{0,1:T(8,128)(2,1)}, u32[]{:S(2)}) copy-start(bf16[128,2880]{0,1:T(8,128)(2,1)} %param.7) | copy-start | bytes 2211844
  7.2 32.2 %all-gather.8.cloned.1.call-start = ((), (), s32[]{:S(2)}) async-start(), calls=%async_computation.8 | async-start | bytes 22118400 | tf_op jit(solution)/shard_map/all_gather | solution.py:74
  7.9 61.4 %all-gather.6.cloned.1.call-start = ((), (), s32[]{:S(2)}) async-start(), calls=%async_computation.7 | async-start | bytes 22118400 | tf_op jit(solution)/shard_map/all_gather | solution.py:75
  8.7 90.6 %all-gather.4.cloned.1.call-start = ((), (), s32[]{:S(2)}) async-start(), calls=%async_computation.6 | async-start | bytes 22118400 | tf_op jit(solution)/shard_map/all_gather | solution.py:76
  11.2 15.1 %all-to-all-start = ((bf16[8,4,2880]{2,1,0:T(4,128)(2,1)}), bf16[8,4,2880]{2,1,0:T(4,128)(2,1)S(1)}, u32[]{:S(2)}, u32[]{:S(2)}) async-start(bf16[8,4,2880]{2,1,0:T(4,128)(2,1)} %copy.32), calls=%async_computation | async-start | bytes 376832 | tf_op jit(solution)/shard_map/all_to_all | solution.py:69
  26.3 11.1 %all-to-all-start.1 = ((bf16[8,4,2880]{2,1,0:T(4,128)(2,1)}), bf16[8,4,2880]{2,1,0:T(4,128)(2,1)S(1)}, u32[]{:S(2)}, u32[]{:S(2)}) async-start(bf16[8,4,2880]{2,1,0:T(4,128)(2,1)} %copy.33), calls=%async_computation.1 | async-start | bytes 376832 | tf_op jit(solution)/shard_map/all_to_all | solution.py:68
  29.7 131.3 %reduce-scatter.4.cloned.1.call-start = ((), (), s32[]{:S(2)}) async-start(), calls=%async_computation.9 | async-start | bytes 22118400 | tf_op jit(solution)/shard_map/reduce_scatter | solution.py:84
  122.0 53.4 %reduce-scatter.6.cloned.1.call-start = ((), (), s32[]{:S(2)}) async-start(), calls=%async_computation.10 | async-start | bytes 22118400 | tf_op jit(solution)/shard_map/reduce_scatter | solution.py:90
  122.6 80.8 %reduce-scatter.8.cloned.1.call-start = ((), (), s32[]{:S(2)}) async-start(), calls=%async_computation.11 | async-start | bytes 22118400 | tf_op jit(solution)/shard_map/reduce_scatter | solution.py:93
  123.2 80.2 %copy-start.1 = (bf16[128,2880]{0,1:T(8,128)(2,1)S(1)}, bf16[128,2880]{0,1:T(8,128)(2,1)}, u32[]{:S(2)}) copy-start(bf16[128,2880]{0,1:T(8,128)(2,1)} %param.8) | copy-start | bytes 2211844
Sparse Core Ops, SparseCore 0:
  9.6 29.7 all-gather.7
  41.0 28.2 all-gather.5
  70.9 28.3 all-gather.3
  122.1 25.2 reduce-scatter.3
  150.1 25.2 reduce-scatter.5
  178.2 25.1 reduce-scatter.7
where the time goes:
time: 211 us; the launch traced here: 210 us
  waiting for transfers between devices  95 us (45%)
  matrix products  73.8 us (35%)
  between operations  14.2 us (7%)
  blocking collectives  13.9 us (7%)
  starting transfers between devices  11.1 us (5%)
    reduce_scatter x1, waiting for transfers between devices, body(): lax.psum_scatter(term_down.astype(jnp.float32).astype(jnp.bfloat16), 'dp'...  27.9 us
    all_gather x1, waiting for transfers between devices, body(): lax.all_gather(up_weight, 'dp', axis=0, tiled=True)  22.1 us
    reduce_scatter x1, waiting for transfers between devices, body(): lax.psum_scatter(term_up.astype(jnp.float32).astype(jnp.bfloat16), 'dp',...  14.4 us
    all_to_all x1, blocking collectives, body(): lax.all_to_all(part_rows.reshape(devices, CAP, model_width), 'expert', sp...  13.9 us
    dot_general x1, matrix products, expert_backward(): jnp.dot(d_up, w_up, preferred_element_type=jnp.float32)  13 us
    all_gather x1, waiting for transfers between devices, body(): lax.all_gather(down_weight, 'dp', axis=0, tiled=True)  11.4 us
    dot_general x1, matrix products, weight_terms(): lax.dot_general(activation, rows_c, contract_first, preferred_element_typ...  10.8 us
    dot_general x1, matrix products, expert_backward(): jnp.dot(d_gate, w_gate, preferred_element_type=jnp.float32)  9.61 us
  transfers between devices with their start and end apart: 8, of which 7 were waited for; matrix products, arithmetic and copies ran while one was open for 25% of the time, Pallas kernels for 0%

commit v1 on v0

--- a/solution.py
+++ b/solution.py
@@ -1,10 +1,338 @@
+import functools
+
 import jax
 import jax.numpy as jnp
 from jax import lax
+from jax.experimental import pallas as pl
+from jax.experimental.pallas import tpu as pltpu
 from jax.sharding import PartitionSpec as P
 
 E_WIN = 8
 CAP = 4
+FOLD = 4
+BLOCK = FOLD * CAP
+LAST = (((1,), (1,)), ((), ()))
+FIRST = (((0,), (0,)), ((), ()))
+F32 = jnp.float32
+BF16 = jnp.bfloat16
+
+
+def fold_columns(width):
+    step = -(-width // (FOLD * 128)) * 128
+    return [(j * step, min(width, (j + 1) * step)) for j in range(FOLD)]
+
+
+def iota(shape, dim):
+    return lax.broadcasted_iota(jnp.int32, shape, dim)
+
+
+def dot(a, b):
+    return jnp.dot(a, b, preferred_element_type=F32)
+
+
+def exchange_kernel(
+    experts, chunk,
+    tok, cot, ids, route, gate_hbm, up_hbm, down_hbm,
+    grad_tok, d_gate_out, d_up_out, act_out, x_out, c_out,
+    gate_w, up_w, down_w, send_x, send_c, recv_x, recv_c, stage,
+    gate_pre, up_pre, total, half_out, half_in, ret_out, ret_in,
+    w_sem, xs_sem, xr_sem, cs_sem, cr_sem, xfs_sem, xfr_sem, cfs_sem, cfr_sem,
+    half_sem, rs_sem, rr_sem,
+):
+    me = lax.axis_index("expert")
+    core = lax.axis_index("dp")
+    peer = 1 - core
+    n_tok, width = tok.shape
+    units = gate_hbm.shape[0]
+    chunks = units // chunk
+    cols = fold_columns(width)
+    lines = experts * BLOCK
+    own_rows = experts * CAP
+    peer_id = {"dp": peer}
+
+    barrier = pltpu.get_barrier_semaphore()
+    for d in range(1, experts):
+        pl.semaphore_signal(
+            barrier, inc=1, device_id={"expert": lax.rem(me + d, experts)},
+            device_id_type=pl.DeviceIdType.MESH,
+        )
+    pl.semaphore_signal(barrier, inc=1, device_id=peer_id, device_id_type=pl.DeviceIdType.MESH)
+
+    def weight_copy(which, c):
+        src = (gate_hbm, up_hbm, down_hbm)[which]
+        dst = (gate_w, up_w, down_w)[which]
+        rows = pl.ds(pl.multiple_of(c * chunk, chunk), chunk)
+        return pltpu.make_async_copy(src.at[rows], dst.at[rows], w_sem.at[which, c])
+
+    for which in range(3):
+        for c in range(chunks):
+            weight_copy(which, c).start()
+
+    line = iota((n_tok, lines), 1)
+    line_expert = line // BLOCK
+    line_slot = (line % CAP).astype(F32)
+    line_fold = (line // CAP) % FOLD
+    member = jnp.zeros((n_tok, lines), F32)
+    weight = jnp.zeros((n_tok, lines), F32)
+    for p in range(ids.shape[1]):
+        hit = ids[:, p : p + 1] == line_expert
+        member += jnp.where(hit, 1.0, 0.0)
+        weight += jnp.where(hit, route[:, p : p + 1], 0.0)
+    earlier = jnp.where(iota((n_tok, n_tok), 0) > iota((n_tok, n_tok), 1), 1.0, 0.0)
+    position = dot(earlier.astype(BF16), member.astype(BF16))
+    place_t = jnp.where(position == line_slot, member, 0.0)
+    place = place_t.T
+    slot_weight = jnp.sum((place_t * weight).T, axis=1, keepdims=True)
+    fold_of = (iota((lines, n_tok), 0) // CAP) % FOLD
+    picks = [jnp.where(fold_of == j, place, 0.0).astype(BF16) for j in range(FOLD)]
+
+    def pack(selects, source):
+        full = dot(selects[0], source[:, cols[0][0] : cols[0][1]])
+        for j in range(1, FOLD - 1):
+            full += dot(selects[j], source[:, cols[j][0] : cols[j][1]])
+        stage[...] = full
+        lo, hi = cols[FOLD - 1]
+        stage[:, : hi - lo] += dot(selects[FOLD - 1], source[:, lo:hi])
+        return stage[...]
+
+    def block(index):
+        return pl.ds(pl.multiple_of(index * BLOCK, BLOCK), BLOCK)
+
+    def slot(src):
+        return block(core * experts + src)
+
+    def row_send(send, recv, s_sem, r_sem, d):
+        to = lax.rem(me + d, experts)
+        return pltpu.make_async_remote_copy(
+            src_ref=send.at[block(to)], dst_ref=recv.at[slot(me)],
+            send_sem=s_sem.at[d], recv_sem=r_sem.at[d],
+            device_id={"expert": to}, device_id_type=pl.DeviceIdType.MESH,
+        )
+
+    def row_arrival(send, recv, s_sem, r_sem, d):
+        origin = lax.rem(me + experts - d, experts)
+        return pltpu.make_async_remote_copy(
+            src_ref=send.at[block(origin)], dst_ref=recv.at[slot(origin)],
+            send_sem=s_sem.at[d], recv_sem=r_sem.at[d],
+            device_id={"expert": origin}, device_id_type=pl.DeviceIdType.MESH,
+        )
+
+    def forward(recv, s_sem, r_sem, d):
+        origin = lax.rem(me + experts - d, experts)
+        return pltpu.make_async_remote_copy(
+            src_ref=recv.at[slot(origin)], dst_ref=recv.at[slot(origin)],
+            send_sem=s_sem.at[d], recv_sem=r_sem.at[d],
+            device_id=peer_id, device_id_type=pl.DeviceIdType.MESH,
+        )
+
+    def forward_arrival(recv, s_sem, r_sem, d):
+        origin = lax.rem(me + experts - d, experts)
+        where = block(peer * experts + origin)
+        return pltpu.make_async_remote_copy(
+            src_ref=recv.at[where], dst_ref=recv.at[where],
+            send_sem=s_sem.at[d], recv_sem=r_sem.at[d],
+            device_id=peer_id, device_id_type=pl.DeviceIdType.MESH,
+        )
+
+    x_sems = (xs_sem, xr_sem)
+    c_sems = (cs_sem, cr_sem)
+    xf_sems = (xfs_sem, xfr_sem)
+    cf_sems = (cfs_sem, cfr_sem)
+    near_last = sorted(range(1, experts), key=lambda d: abs(2 * d - experts))
+
+    send_x[...] = pack(picks, tok).astype(BF16)
+    recv_x[slot(me), :] = send_x[block(me), :]
+    pl.semaphore_wait(barrier, experts)
+    for d in near_last:
+        row_send(send_x, recv_x, *x_sems, d).start()
+    forward(recv_x, *xf_sems, 0).start()
+    send_c[...] = (pack(picks, cot) * slot_weight).astype(BF16)
+    recv_c[slot(me), :] = send_c[block(me), :]
+    for d in near_last:
+        row_send(send_c, recv_c, *c_sems, d).start()
+    forward(recv_c, *cf_sems, 0).start()
+
+    all_rows = 2 * own_rows
+    row = iota((all_rows, 2 * lines), 0)
+    line_of = iota((all_rows, 2 * lines), 1)
+    base = (row // CAP) * BLOCK + row % CAP
+
+    def unpack(recv, out):
+        for j, (lo, hi) in enumerate(cols):
+            select = jnp.where(line_of == base + j * CAP, 1.0, 0.0).astype(BF16)
+            out[:, lo:hi] = dot(select, recv[:, : hi - lo]).astype(BF16)
+
+    def gather(send, recv, sems, f_sems, out):
+        for d in near_last[::-1]:
+            row_arrival(send, recv, *sems, d).wait_recv()
+            forward(recv, *f_sems, d).start()
+        for d in range(experts):
+            forward_arrival(recv, *f_sems, d).wait_recv()
+        unpack(recv, out)
+
+    gather(send_x, recv_x, x_sems, xf_sems, x_out)
+
+    def span(c):
+        return pl.ds(pl.multiple_of(c * chunk, chunk), chunk)
+
+    def project(c, carry):
+        weight_copy(0, c).wait()
+        weight_copy(1, c).wait()
+        x = x_out[...]
+        gate_pre[:, span(c)] = lax.dot_general(x, gate_w[span(c), :], LAST, preferred_element_type=F32)
+        up_pre[:, span(c)] = lax.dot_general(x, up_w[span(c), :], LAST, preferred_element_type=F32)
+        return carry
+
+    lax.fori_loop(0, chunks, project, 0)
+    gather(send_c, recv_c, c_sems, cf_sems, c_out)
+
+    total[...] = jnp.zeros_like(total)
+
+    def backward(c, carry):
+        weight_copy(2, c).wait()
+        d_act = lax.dot_general(
+            c_out[...], down_w[span(c), :], LAST, preferred_element_type=F32
+        )
+        gate = gate_pre[:, span(c)]
+        up = up_pre[:, span(c)] + 1.0
+        sig = jax.nn.sigmoid(1.702 * gate)
+        gated = gate * sig
+        act_out[:, span(c)] = (up * gated).astype(BF16)
+        d_up = (d_act * gated).astype(BF16)
+        d_gate = (d_act * up * (sig + 1.702 * gate * sig * (1.0 - sig))).astype(BF16)
+        d_up_out[:, span(c)] = d_up
+        d_gate_out[:, span(c)] = d_gate
+        total[...] += dot(d_gate, gate_w[span(c), :]) + dot(d_up, up_w[span(c), :])
+        return carry
+
+    lax.fori_loop(0, chunks, backward, 0)
+
+    def half_rows(which):
+        return pl.ds(pl.multiple_of(which * own_rows, own_rows), own_rows)
+
+    half_out[...] = total[half_rows(peer), :].astype(BF16)
+    swap = pltpu.make_async_remote_copy(
+        src_ref=half_out, dst_ref=half_in, send_sem=half_sem.at[0], recv_sem=half_sem.at[1],
+        device_id=peer_id, device_id_type=pl.DeviceIdType.MESH,
+    )
+    swap.start()
+    swap.wait()
+    half_out[...] = (total[half_rows(core), :] + half_in[...].astype(F32)).astype(BF16)
+
+    out_line = iota((lines, own_rows), 0)
+    wanted = (out_line // BLOCK) * CAP + out_line % CAP
+    matched = wanted == iota((lines, own_rows), 1)
+    out_fold = (out_line // CAP) % FOLD
+    puts = [
+        jnp.where(jnp.logical_and(matched, out_fold == j), 1.0, 0.0).astype(BF16)
+        for j in range(FOLD)
+    ]
+    ret_out[...] = pack(puts, half_out).astype(BF16)
+    ret_in[block(me), :] = ret_out[block(me), :]
+
+    def ret_copy(d, sending):
+        other = lax.rem(me + d, experts) if sending else lax.rem(me + experts - d, experts)
+        return pltpu.make_async_remote_copy(
+            src_ref=ret_out.at[block(other)], dst_ref=ret_in.at[block(me if sending else other)],
+            send_sem=rs_sem.at[d], recv_sem=rr_sem.at[d],
+            device_id={"expert": other}, device_id_type=pl.DeviceIdType.MESH,
+        )
+
+    for d in near_last:
+        ret_copy(d, True).start()
+    for d in range(1, experts):
+        row_send(send_x, recv_x, *x_sems, d).wait_send()
+        row_send(send_c, recv_c, *c_sems, d).wait_send()
+    for d in range(experts):
+        forward(recv_x, *xf_sems, d).wait_send()
+        forward(recv_c, *cf_sems, d).wait_send()
+    for d in range(1, experts):
+        ret_copy(d, False).wait_recv()
+    for j, (lo, hi) in enumerate(cols):
+        take = jnp.where(line_fold == j, place_t, 0.0).astype(BF16)
+        grad_tok[:, lo:hi] = dot(take, ret_in[:, : hi - lo]).astype(BF16)
+    for d in range(1, experts):
+        ret_copy(d, True).wait_send()
+
+
+def weight_kernel(d_gate, d_up, act, x, c, g_gate, g_up, g_down):
+    def term(a, b):
+        return lax.dot_general(a[...], b[...], FIRST, preferred_element_type=F32).astype(BF16)
+
+    g_gate[...] = term(d_gate, x)
+    g_up[...] = term(d_up, x)
+    g_down[...] = term(act, c)
+
+
+def kernel_body(tokens, cotangent, expert_ids, route_weight, gate_weight, up_weight, down_weight):
+    experts = lax.axis_size("expert")
+    n_tok, width = tokens.shape
+    units = gate_weight.shape[0]
+    chunk = 256
+    rows = 2 * experts * CAP
+    lines = experts * BLOCK
+    lo, hi = fold_columns(width)[0]
+    fold_width = hi - lo
+    vmem = pl.BlockSpec(memory_space=pltpu.VMEM)
+    hbm = pl.BlockSpec(memory_space=pl.ANY)
+    sem = pltpu.SemaphoreType.DMA
+    shape = jax.ShapeDtypeStruct
+    grad_tokens, d_gate, d_up, act, x, c = pl.pallas_call(
+        functools.partial(exchange_kernel, experts, chunk),
+        out_shape=(
+            shape((n_tok, width), BF16),
+            shape((rows, units), BF16),
+            shape((rows, units), BF16),
+            shape((rows, units), BF16),
+            shape((rows, width), BF16),
+            shape((rows, width), BF16),
+        ),
+        in_specs=[vmem] * 4 + [hbm] * 3,
+        out_specs=(vmem,) * 6,
+        scratch_shapes=[
+            pltpu.VMEM((units, width), BF16),
+            pltpu.VMEM((units, width), BF16),
+            pltpu.VMEM((units, width), BF16),
+            pltpu.VMEM((lines, fold_width), BF16),
+            pltpu.VMEM((lines, fold_width), BF16),
+            pltpu.VMEM((2 * lines, fold_width), BF16),
+            pltpu.VMEM((2 * lines, fold_width), BF16),
+            pltpu.VMEM((lines, fold_width), F32),
+            pltpu.VMEM((rows, units), F32),
+            pltpu.VMEM((rows, units), F32),
+            pltpu.VMEM((rows, width), F32),
+            pltpu.VMEM((rows // 2, width), BF16),
+            pltpu.VMEM((rows // 2, width), BF16),
+            pltpu.VMEM((lines, fold_width), BF16),
+            pltpu.VMEM((lines, fold_width), BF16),
+            sem((3, units // chunk)),
+            sem((experts,)), sem((experts,)), sem((experts,)), sem((experts,)),
+            sem((experts,)), sem((experts,)), sem((experts,)), sem((experts,)),
+            sem((2,)), sem((experts,)), sem((experts,)),
+        ],
+        compiler_params=pltpu.CompilerParams(
+            collective_id=0, has_side_effects=True, vmem_limit_bytes=56 * 1024 * 1024
+        ),
+        name="exchange",
+    )(tokens, cotangent, expert_ids, route_weight, gate_weight, up_weight, down_weight)
+
+    step = 128
+    part = pl.BlockSpec((rows, step), lambda i: (0, i))
+    whole = pl.BlockSpec((rows, width), lambda i: (0, 0))
+    result = pl.BlockSpec((step, width), lambda i: (i, 0))
+    grads = pl.pallas_call(
+        weight_kernel,
+        out_shape=(shape((units, width), BF16),) * 3,
+        grid=(units // step,),
+        in_specs=[part, part, part, whole, whole],
+        out_specs=(result,) * 3,
+        compiler_params=pltpu.CompilerParams(vmem_limit_bytes=32 * 1024 * 1024),
+        cost_estimate=pl.CostEstimate(
+            flops=6 * rows * units * width, bytes_accessed=6 * units * width, transcendentals=0
+        ),
+        name="weight_grads",
+    )(d_gate, d_up, act, x, c)
+    return (grad_tokens, *grads)
 
 
 def expert_backward(rows_x, rows_c, w_gate, w_up, w_down):
@@ -117,8 +445,9 @@
 
 
 def solution(mesh):
+    sizes = mesh.shape
     return jax.shard_map(
-        body,
+        kernel_body if sizes["expert"] == E_WIN and sizes["dp"] == 2 else body,
         mesh=mesh,
         in_specs=(
             P(("groups", "expert", "dp"), None),

time: 211 us -> 138 us (0.65)
  waiting for transfers between devices: 95 us -> 0 us
  local copies, waits for them, and re-layouts: 1.98 us -> 82.6 us
  matrix products: 73.8 us -> 0 us
  Pallas kernels: 0 us -> 52.5 us
  blocking collectives: 13.9 us -> 0 us
  between operations: 14.2 us -> 0.65 us
  starting transfers between devices: 11.1 us -> 0 us
    unnamed x10 -> x25, local copies, waits for them, and re-layouts: 0.03 us -> 82.6 us
    dot_general x12 -> x0, matrix products: 73.8 us -> none  [the longest x1 13 us: expert_backward(): jnp.dot(d_up, w_up, preferred_element_type=jnp.float32)]
    pallas_call x0 -> x2, Pallas kernels: none -> 52.5 us  [the longest x1 43.3 us: kernel_body(): pl.pallas_call(functools.partial(exchange_kernel, experts, chunk), out_sh...]
    reduce_scatter x3 -> x0, waiting for transfers between devices: 42.3 us -> none  [the longest x1 27.9 us: body(): lax.psum_scatter(term_down.astype(jnp.float32).astype(jnp.bfloat16), 'dp'...]
    all_gather x3 -> x0, waiting for transfers between devices: 35.5 us -> none  [the longest x1 22.1 us: body(): lax.all_gather(up_weight, 'dp', axis=0, tiled=True)]
    all_to_all x2 -> x0, waiting for transfers between devices: 14.2 us -> none  [the longest x1 7.53 us: body(): lax.all_to_all(send_x, 'expert', split_axis=0, concat_axis=0, tiled=True)]
    all_to_all x1 -> x0, blocking collectives: 13.9 us -> none  [body(): lax.all_to_all(part_rows.reshape(devices, CAP, model_width), 'expert', sp...]
    all_to_all x2 -> x0, starting transfers between devices: 10.7 us -> none  [the longest x1 7.25 us: body(): lax.all_to_all(send_c, 'expert', split_axis=0, concat_axis=0, tiled=True)]
  transfers between devices with their start and end apart: 8 -> 0, of which waited for: 7 -> 0; matrix products, arithmetic and copies ran while one was open for 25% -> 0% of each run, Pallas kernels for 0% -> 0%
where the time goes in v1:
time: 138 us; the launch traced here: 136 us
  local copies, waits for them, and re-layouts  82.6 us (60%)
  Pallas kernels  52.5 us (38%)
    unnamed x25, local copies, waits for them, and re-layouts  82.6 us
    pallas_call x1, Pallas kernels, kernel_body(): pl.pallas_call(functools.partial(exchange_kernel, experts, chunk), out_sh...  43.3 us
    pallas_call x1, Pallas kernels, kernel_body(): pl.pallas_call(weight_kernel, out_shape=(shape((units, width), BF16),) *...  9.17 us

profile of v1, /device:TPU:0, one launch (start us, length us, event | category | flops | bytes accessed | tf_op | source)
XLA Modules:
  0.0 135.7 jit_solution(3883782317410426527)
XLA Ops:
  0.6 1.4 %copy.13.ids = s32[128,4]{1,0:T(8,128)} copy(s32[128,4]{0,1:T(4,128)} %param.9) | data formatting | bytes 4096 | tf_op args[2]
  2.0 1.4 %copy.14.route = f32[128,4]{1,0:T(8,128)} copy(f32[128,4]{0,1:T(4,128)} %param.10) | data formatting | bytes 4096 | tf_op args[3]
  3.5 2.3 %copy.11.tok = bf16[128,2880]{1,0:T(8,128)(2,1)} copy(bf16[128,2880]{0,1:T(8,128)(2,1)} %param.7) | data formatting | bytes 1474560 | tf_op args[0]
  5.7 2.3 %copy.12.cot = bf16[128,2880]{1,0:T(8,128)(2,1)} copy(bf16[128,2880]{0,1:T(8,128)(2,1)} %param.8) | data formatting | bytes 1474560 | tf_op args[1]
  8.0 10.4 %copy.15.gate_hbm = bf16[1280,2880]{1,0:T(8,128)(2,1)} copy(bf16[1280,2880]{0,1:T(8,128)(2,1)} %param.11) | data formatting | bytes 14745600 | tf_op args[4]
  18.4 10.5 %copy.16.up_hbm = bf16[1280,2880]{1,0:T(8,128)(2,1)} copy(bf16[1280,2880]{0,1:T(8,128)(2,1)} %param.12) | data formatting | bytes 14745600 | tf_op args[5]
  28.9 10.5 %copy.17.down_hbm = bf16[1280,2880]{1,0:T(8,128)(2,1)} copy(bf16[1280,2880]{0,1:T(8,128)(2,1)} %param.13) | data formatting | bytes 14745600 | tf_op args[6]
  39.3 43.3 %exchange.1 = (bf16[128,2880]{1,0:T(8,128)(2,1)}, bf16[64,1280]{1,0:T(8,128)(2,1)}, bf16[64,1280]{1,0:T(8,128)(2,1)}, bf16[64,1280]{1,0:T(8,128)(2,1)}, bf16[64,...) custom-call(bf16[128,2880]{1,0:T(8,128)(2,1)} %copy.11.tok, bf16[128,2880]{1,0:T(8,128)(2,1)} %copy.12.cot, ...), custom_call_target="tpu_custom_call" | custom-call | tf_op jit(solution)/shard_map/exchange/pallas_call | solution.py:280
  82.7 2.3 %copy.18 = bf16[128,2880]{0,1:T(8,128)(2,1)} copy(bf16[128,2880]{1,0:T(8,128)(2,1)} %get-tuple-element.22) | data formatting | bytes 1474560
  84.9 0.0 copy-start.2
  84.9 1.0 copy-done.2
  85.9 0.0 copy-start.3
  85.9 1.0 copy-done.3
  86.9 0.0 copy-start.4
  86.9 0.9 copy-done.4
  87.8 0.0 copy-start.5
  87.8 0.9 copy-done.5
  88.8 0.0 copy-start.6
  88.8 0.9 copy-done.6
  89.7 9.2 %weight_grads.1 = (bf16[1280,2880]{1,0:T(8,128)(2,1)S(1)}, bf16[1280,2880]{1,0:T(8,128)(2,1)S(1)}, bf16[1280,2880]{1,0:T(8,128)(2,1)}) custom-call(bf16[64,1280]{1,0:T(8,128)(2,1)S(1)} %copy-done.4, bf16[64,1280]{1,0:T(8,128)(2,1)S(1)} %copy-done.5, bf16[64,1280]{1,0:T(8,128)(2,1)S(1)} %copy-done.6, bf16[64,2880]{1,0:T(8,128)(2,1)S(1)} %copy-done.2, ...), custom_call_target="tpu_custom_call" | custom-call | flops 1415577600 | bytes 22118400 | tf_op jit(solution)/shard_map/weight_grads/pallas_call | solution.py:323
  98.8 0.0 copy-start
  98.8 3.0 %copy-done = bf16[1280,2880]{1,0:T(8,128)(2,1)} copy-done((bf16[1280,2880]{1,0:T(8,128)(2,1)}, bf16[1280,2880]{1,0:T(8,128)(2,1)S(1)}, u32[]{:S(2)}) %copy-start) | copy-done | bytes 7372824
  101.9 0.0 copy-start.1
  101.9 3.0 %copy-done.1 = bf16[1280,2880]{1,0:T(8,128)(2,1)} copy-done((bf16[1280,2880]{1,0:T(8,128)(2,1)}, bf16[1280,2880]{1,0:T(8,128)(2,1)S(1)}, u32[]{:S(2)}) %copy-start.1) | copy-done | bytes 7372824
  104.9 10.3 %copy.19 = bf16[1280,2880]{0,1:T(8,128)(2,1)} copy(bf16[1280,2880]{1,0:T(8,128)(2,1)} %copy-done.1) | data formatting | bytes 14745600
  115.2 10.3 %copy.20 = bf16[1280,2880]{0,1:T(8,128)(2,1)} copy(bf16[1280,2880]{1,0:T(8,128)(2,1)} %copy-done) | data formatting | bytes 14745600
  125.4 10.3 %copy.21 = bf16[1280,2880]{0,1:T(8,128)(2,1)} copy(bf16[1280,2880]{1,0:T(8,128)(2,1)} %get-tuple-element.25) | data formatting | bytes 14745600
Async XLA Ops:
  84.9 1.0 copy-start.2
  85.9 1.0 copy-start.3
  86.9 0.9 copy-start.4
  87.8 0.9 copy-start.5
  88.8 0.9 copy-start.6
  98.8 3.0 %copy-start = (bf16[1280,2880]{1,0:T(8,128)(2,1)}, bf16[1280,2880]{1,0:T(8,128)(2,1)S(1)}, u32[]{:S(2)}) copy-start(bf16[1280,2880]{1,0:T(8,128)(2,1)S(1)} %get-tuple-element.24) | copy-start | bytes 22118404
  101.9 3.0 %copy-start.1 = (bf16[1280,2880]{1,0:T(8,128)(2,1)}, bf16[1280,2880]{1,0:T(8,128)(2,1)S(1)}, u32[]{:S(2)}) copy-start(bf16[1280,2880]{1,0:T(8,128)(2,1)S(1)} %get-tuple-element.23) | copy-start | bytes 22118404

commit v2 on v1

--- a/solution.py
+++ b/solution.py
@@ -42,8 +42,8 @@
     me = lax.axis_index("expert")
     core = lax.axis_index("dp")
     peer = 1 - core
-    n_tok, width = tok.shape
-    units = gate_hbm.shape[0]
+    width, n_tok = tok.shape
+    units = gate_hbm.shape[1]
     chunks = units // chunk
     cols = fold_columns(width)
     lines = experts * BLOCK
@@ -62,38 +62,41 @@
         src = (gate_hbm, up_hbm, down_hbm)[which]
         dst = (gate_w, up_w, down_w)[which]
         rows = pl.ds(pl.multiple_of(c * chunk, chunk), chunk)
-        return pltpu.make_async_copy(src.at[rows], dst.at[rows], w_sem.at[which, c])
+        return pltpu.make_async_copy(src.at[:, rows], dst.at[:, rows], w_sem.at[which, c])
 
     for which in range(3):
         for c in range(chunks):
             weight_copy(which, c).start()
 
-    line = iota((n_tok, lines), 1)
+    line = iota((lines, n_tok), 0)
     line_expert = line // BLOCK
     line_slot = (line % CAP).astype(F32)
     line_fold = (line // CAP) % FOLD
-    member = jnp.zeros((n_tok, lines), F32)
-    weight = jnp.zeros((n_tok, lines), F32)
-    for p in range(ids.shape[1]):
-        hit = ids[:, p : p + 1] == line_expert
+    member = jnp.zeros((lines, n_tok), F32)
+    weight = jnp.zeros((lines, n_tok), F32)
+    for p in range(ids.shape[0]):
+        hit = ids[p : p + 1, :] == line_expert
         member += jnp.where(hit, 1.0, 0.0)
-        weight += jnp.where(hit, route[:, p : p + 1], 0.0)
-    earlier = jnp.where(iota((n_tok, n_tok), 0) > iota((n_tok, n_tok), 1), 1.0, 0.0)
-    position = dot(earlier.astype(BF16), member.astype(BF16))
-    place_t = jnp.where(position == line_slot, member, 0.0)
-    place = place_t.T
-    slot_weight = jnp.sum((place_t * weight).T, axis=1, keepdims=True)
-    fold_of = (iota((lines, n_tok), 0) // CAP) % FOLD
-    picks = [jnp.where(fold_of == j, place, 0.0).astype(BF16) for j in range(FOLD)]
-
-    def pack(selects, source):
-        full = dot(selects[0], source[:, cols[0][0] : cols[0][1]])
+        weight += jnp.where(hit, route[p : p + 1, :], 0.0)
+    earlier = jnp.where(iota((n_tok, n_tok), 0) < iota((n_tok, n_tok), 1), 1.0, 0.0)
+    position = dot(member.astype(BF16), earlier.astype(BF16))
+    place = jnp.where(position == line_slot, member, 0.0)
+    slot_weight = jnp.sum(place * weight, axis=1, keepdims=True)
+    picks = [jnp.where(line_fold == j, place, 0.0).astype(BF16) for j in range(FOLD)]
+
+    def pack(selects, columns):
+        full = columns(selects[0], *cols[0])
         for j in range(1, FOLD - 1):
-            full += dot(selects[j], source[:, cols[j][0] : cols[j][1]])
+            full += columns(selects[j], *cols[j])
         stage[...] = full
         lo, hi = cols[FOLD - 1]
-        stage[:, : hi - lo] += dot(selects[FOLD - 1], source[:, lo:hi])
+        stage[:, : hi - lo] += columns(selects[FOLD - 1], lo, hi)
         return stage[...]
+
+    def from_tokens(source):
+        return lambda select, lo, hi: lax.dot_general(
+            select, source[lo:hi, :], LAST, preferred_element_type=F32
+        )
 
     def block(index):
         return pl.ds(pl.multiple_of(index * BLOCK, BLOCK), BLOCK)
@@ -140,13 +143,13 @@
     cf_sems = (cfs_sem, cfr_sem)
     near_last = sorted(range(1, experts), key=lambda d: abs(2 * d - experts))
 
-    send_x[...] = pack(picks, tok).astype(BF16)
+    send_x[...] = pack(picks, from_tokens(tok)).astype(BF16)
     recv_x[slot(me), :] = send_x[block(me), :]
     pl.semaphore_wait(barrier, experts)
     for d in near_last:
         row_send(send_x, recv_x, *x_sems, d).start()
     forward(recv_x, *xf_sems, 0).start()
-    send_c[...] = (pack(picks, cot) * slot_weight).astype(BF16)
+    send_c[...] = (pack(picks, from_tokens(cot)) * slot_weight).astype(BF16)
     recv_c[slot(me), :] = send_c[block(me), :]
     for d in near_last:
         row_send(send_c, recv_c, *c_sems, d).start()
@@ -179,8 +182,8 @@
         weight_copy(0, c).wait()
         weight_copy(1, c).wait()
         x = x_out[...]
-        gate_pre[:, span(c)] = lax.dot_general(x, gate_w[span(c), :], LAST, preferred_element_type=F32)
-        up_pre[:, span(c)] = lax.dot_general(x, up_w[span(c), :], LAST, preferred_element_type=F32)
+        gate_pre[:, span(c)] = dot(x, gate_w[:, span(c)])
+        up_pre[:, span(c)] = dot(x, up_w[:, span(c)])
         return carry
 
     lax.fori_loop(0, chunks, project, 0)
@@ -190,9 +193,7 @@
 
     def backward(c, carry):
         weight_copy(2, c).wait()
-        d_act = lax.dot_general(
-            c_out[...], down_w[span(c), :], LAST, preferred_element_type=F32
-        )
+        d_act = dot(c_out[...], down_w[:, span(c)])
         gate = gate_pre[:, span(c)]
         up = up_pre[:, span(c)] + 1.0
         sig = jax.nn.sigmoid(1.702 * gate)
@@ -202,7 +203,9 @@
         d_gate = (d_act * up * (sig + 1.702 * gate * sig * (1.0 - sig))).astype(BF16)
         d_up_out[:, span(c)] = d_up
         d_gate_out[:, span(c)] = d_gate
-        total[...] += dot(d_gate, gate_w[span(c), :]) + dot(d_up, up_w[span(c), :])
+        total[...] += lax.dot_general(
+            d_gate, gate_w[:, span(c)], LAST, preferred_element_type=F32
+        ) + lax.dot_general(d_up, up_w[:, span(c)], LAST, preferred_element_type=F32)
         return carry
 
     lax.fori_loop(0, chunks, backward, 0)
@@ -227,7 +230,7 @@
         jnp.where(jnp.logical_and(matched, out_fold == j), 1.0, 0.0).astype(BF16)
         for j in range(FOLD)
     ]
-    ret_out[...] = pack(puts, half_out).astype(BF16)
+    ret_out[...] = pack(puts, lambda select, lo, hi: dot(select, half_out[:, lo:hi])).astype(BF16)
     ret_in[block(me), :] = ret_out[block(me), :]
 
     def ret_copy(d, sending):
@@ -249,8 +252,9 @@
     for d in range(1, experts):
         ret_copy(d, False).wait_recv()
     for j, (lo, hi) in enumerate(cols):
-        take = jnp.where(line_fold == j, place_t, 0.0).astype(BF16)
-        grad_tok[:, lo:hi] = dot(take, ret_in[:, : hi - lo]).astype(BF16)
+        grad_tok[lo:hi, :] = lax.dot_general(
+            ret_in[:, : hi - lo], picks[j], FIRST, preferred_element_type=F32
+        ).astype(BF16)
     for d in range(1, experts):
         ret_copy(d, True).wait_send()
 
@@ -259,9 +263,9 @@
     def term(a, b):
         return lax.dot_general(a[...], b[...], FIRST, preferred_element_type=F32).astype(BF16)
 
-    g_gate[...] = term(d_gate, x)
-    g_up[...] = term(d_up, x)
-    g_down[...] = term(act, c)
+    g_gate[...] = term(x, d_gate)
+    g_up[...] = term(x, d_up)
+    g_down[...] = term(c, act)
 
 
 def kernel_body(tokens, cotangent, expert_ids, route_weight, gate_weight, up_weight, down_weight):
@@ -280,7 +284,7 @@
     grad_tokens, d_gate, d_up, act, x, c = pl.pallas_call(
         functools.partial(exchange_kernel, experts, chunk),
         out_shape=(
-            shape((n_tok, width), BF16),
+            shape((width, n_tok), BF16),
             shape((rows, units), BF16),
             shape((rows, units), BF16),
             shape((rows, units), BF16),
@@ -290,9 +294,9 @@
         in_specs=[vmem] * 4 + [hbm] * 3,
         out_specs=(vmem,) * 6,
         scratch_shapes=[
-            pltpu.VMEM((units, width), BF16),
-            pltpu.VMEM((units, width), BF16),
-            pltpu.VMEM((units, width), BF16),
+            pltpu.VMEM((width, units), BF16),
+            pltpu.VMEM((width, units), BF16),
+            pltpu.VMEM((width, units), BF16),
             pltpu.VMEM((lines, fold_width), BF16),
             pltpu.VMEM((lines, fold_width), BF16),
             pltpu.VMEM((2 * lines, fold_width), BF16),
@@ -314,17 +318,20 @@
             collective_id=0, has_side_effects=True, vmem_limit_bytes=56 * 1024 * 1024
         ),
         name="exchange",
-    )(tokens, cotangent, expert_ids, route_weight, gate_weight, up_weight, down_weight)
-
-    step = 128
+    )(
+        tokens.T, cotangent.T, expert_ids.T, route_weight.T,
+        gate_weight.T, up_weight.T, down_weight.T,
+    )
+
+    step = 384
     part = pl.BlockSpec((rows, step), lambda i: (0, i))
-    whole = pl.BlockSpec((rows, width), lambda i: (0, 0))
-    result = pl.BlockSpec((step, width), lambda i: (i, 0))
+    whole = pl.BlockSpec((rows, units), lambda i: (0, 0))
+    result = pl.BlockSpec((step, units), lambda i: (i, 0))
     grads = pl.pallas_call(
         weight_kernel,
-        out_shape=(shape((units, width), BF16),) * 3,
-        grid=(units // step,),
-        in_specs=[part, part, part, whole, whole],
+        out_shape=(shape((width, units), BF16),) * 3,
+        grid=(pl.cdiv(width, step),),
+        in_specs=[whole, whole, whole, part, part],
         out_specs=(result,) * 3,
         compiler_params=pltpu.CompilerParams(vmem_limit_bytes=32 * 1024 * 1024),
         cost_estimate=pl.CostEstimate(
@@ -332,7 +339,7 @@
         ),
         name="weight_grads",
     )(d_gate, d_up, act, x, c)
-    return (grad_tokens, *grads)
+    return (grad_tokens.T, *(g.T for g in grads))
 
 
 def expert_backward(rows_x, rows_c, w_gate, w_up, w_down):

time: 138 us -> 59.1 us (0.43); the launches traced: 136 us -> 58.7 us
  local copies, waits for them, and re-layouts: 82.6 us -> 6.74 us
    unnamed x25 -> x11, local copies, waits for them, and re-layouts: 82.6 us -> 6.74 us
    pallas_call x1, Pallas kernels: 43.3 us -> 40.5 us  [kernel_body(): pl.pallas_call(functools.partial(exchange_kernel, experts, chunk), out_sh...]
    pallas_call x1, Pallas kernels: 9.17 us -> 10.8 us  [kernel_body(): pl.pallas_call(weight_kernel, out_shape=(shape((width, units), BF16),) *...]
where the time goes in v2:
time: 59.1 us; the launch traced here: 58.7 us
  Pallas kernels  51.3 us (87%)
  local copies, waits for them, and re-layouts  6.74 us (11%)
  between operations  0.65 us (1%)
    pallas_call x1, Pallas kernels, kernel_body(): pl.pallas_call(functools.partial(exchange_kernel, experts, chunk), out_sh...  40.5 us
    pallas_call x1, Pallas kernels, kernel_body(): pl.pallas_call(weight_kernel, out_shape=(shape((width, units), BF16),) *...  10.8 us
    unnamed x11, local copies, waits for them, and re-layouts  6.74 us

profile of v2, /device:TPU:0, one launch (start us, length us, event | category | flops | bytes accessed | tf_op | source)
XLA Modules:
  0.0 58.7 jit_solution(14868639610923656890)
XLA Ops:
  0.6 40.5 %exchange.1 = (bf16[2880,128]{1,0:T(8,128)(2,1)}, bf16[64,1280]{1,0:T(8,128)(2,1)}, bf16[64,1280]{1,0:T(8,128)(2,1)}, bf16[64,1280]{1,0:T(8,128)(2,1)}, bf16[64,...) custom-call(bf16[2880,128]{1,0:T(8,128)(2,1)} %bitcast.14, bf16[2880,128]{1,0:T(8,128)(2,1)} %bitcast.15, s32[4,128]{1,0:T(4,128)} %bitcast.17, ...), custom_call_target="tpu_custom_call" | custom-call | tf_op jit(solution)/shard_map/exchange/pallas_call | solution.py:284
  41.1 0.0 copy-start
  41.1 1.0 %copy-done = bf16[64,2880]{1,0:T(8,128)(2,1)S(1)} copy-done((bf16[64,2880]{1,0:T(8,128)(2,1)S(1)}, bf16[64,2880]{1,0:T(8,128)(2,1)}, u32[]{:S(2)}) %copy-start) | copy-done | bytes 368664
  42.1 0.0 copy-start.1
  42.1 1.0 %copy-done.1 = bf16[64,2880]{1,0:T(8,128)(2,1)S(1)} copy-done((bf16[64,2880]{1,0:T(8,128)(2,1)S(1)}, bf16[64,2880]{1,0:T(8,128)(2,1)}, u32[]{:S(2)}) %copy-start.1) | copy-done | bytes 368664
  43.1 0.0 copy-start.2
  43.1 0.9 %copy-done.2 = bf16[64,1280]{1,0:T(8,128)(2,1)S(1)} copy-done((bf16[64,1280]{1,0:T(8,128)(2,1)S(1)}, bf16[64,1280]{1,0:T(8,128)(2,1)}, u32[]{:S(2)}) %copy-start.2) | copy-done | bytes 163864
  44.0 0.0 copy-start.3
  44.0 0.9 %copy-done.3 = bf16[64,1280]{1,0:T(8,128)(2,1)S(1)} copy-done((bf16[64,1280]{1,0:T(8,128)(2,1)S(1)}, bf16[64,1280]{1,0:T(8,128)(2,1)}, u32[]{:S(2)}) %copy-start.3) | copy-done | bytes 163864
  44.9 0.0 copy-start.4
  45.0 0.9 %copy-done.4 = bf16[64,1280]{1,0:T(8,128)(2,1)S(1)} copy-done((bf16[64,1280]{1,0:T(8,128)(2,1)S(1)}, bf16[64,1280]{1,0:T(8,128)(2,1)}, u32[]{:S(2)}) %copy-start.4) | copy-done | bytes 163864
  45.9 10.8 %weight_grads.1 = (bf16[2880,1280]{1,0:T(8,128)(2,1)}, bf16[2880,1280]{1,0:T(8,128)(2,1)}, bf16[2880,1280]{1,0:T(8,128)(2,1)}) custom-call(bf16[64,1280]{1,0:T(8,128)(2,1)S(1)} %copy-done.2, bf16[64,1280]{1,0:T(8,128)(2,1)S(1)} %copy-done.3, bf16[64,1280]{1,0:T(8,128)(2,1)S(1)} %copy-done.4, bf16[64,2880]{1,0:T(8,128)(2,1)S(1)} %copy-done, ...), custom_call_target="tpu_custom_call" | custom-call | flops 1415577600 | bytes 22118400 | tf_op jit(solution)/shard_map/weight_grads/pallas_call | solution.py:330
  56.7 2.0 %copy.12 = bf16[128,2880]{0,1:T(8,128)(2,1)} copy(bf16[128,2880]{0,1:T(8,128)(2,1)} %bitcast.16) | data formatting | bytes 1474560
Async XLA Ops:
  41.1 1.0 %copy-start = (bf16[64,2880]{1,0:T(8,128)(2,1)S(1)}, bf16[64,2880]{1,0:T(8,128)(2,1)}, u32[]{:S(2)}) copy-start(bf16[64,2880]{1,0:T(8,128)(2,1)} %get-tuple-element.17.x) | copy-start | bytes 1105924
  42.1 1.0 %copy-start.1 = (bf16[64,2880]{1,0:T(8,128)(2,1)S(1)}, bf16[64,2880]{1,0:T(8,128)(2,1)}, u32[]{:S(2)}) copy-start(bf16[64,2880]{1,0:T(8,128)(2,1)} %get-tuple-element.18.c) | copy-start | bytes 1105924
  43.1 0.9 %copy-start.2 = (bf16[64,1280]{1,0:T(8,128)(2,1)S(1)}, bf16[64,1280]{1,0:T(8,128)(2,1)}, u32[]{:S(2)}) copy-start(bf16[64,1280]{1,0:T(8,128)(2,1)} %get-tuple-element.14.d_gate) | copy-start | bytes 491524
  44.0 0.9 %copy-start.3 = (bf16[64,1280]{1,0:T(8,128)(2,1)S(1)}, bf16[64,1280]{1,0:T(8,128)(2,1)}, u32[]{:S(2)}) copy-start(bf16[64,1280]{1,0:T(8,128)(2,1)} %get-tuple-element.15.d_up) | copy-start | bytes 491524
  44.9 0.9 %copy-start.4 = (bf16[64,1280]{1,0:T(8,128)(2,1)S(1)}, bf16[64,1280]{1,0:T(8,128)(2,1)}, u32[]{:S(2)}) copy-start(bf16[64,1280]{1,0:T(8,128)(2,1)} %get-tuple-element.16.act) | copy-start | bytes 491524

commit v3 on v2

--- a/solution.py
+++ b/solution.py
@@ -333,7 +333,7 @@
         grid=(pl.cdiv(width, step),),
         in_specs=[whole, whole, whole, part, part],
         out_specs=(result,) * 3,
-        compiler_params=pltpu.CompilerParams(vmem_limit_bytes=32 * 1024 * 1024),
+        compiler_params=pltpu.CompilerParams(vmem_limit_bytes=56 * 1024 * 1024),
         cost_estimate=pl.CostEstimate(
             flops=6 * rows * units * width, bytes_accessed=6 * units * width, transcendentals=0
         ),

time: 59.1 us -> 55.1 us (0.932)
  local copies, waits for them, and re-layouts: 6.74 us -> 2.03 us
  Pallas kernels: 51.3 us -> 52.2 us
    unnamed x11 -> x1, local copies, waits for them, and re-layouts: 6.74 us -> 2.03 us
    pallas_call x1, Pallas kernels: 10.8 us -> 11.8 us  [kernel_body(): pl.pallas_call(weight_kernel, out_shape=(shape((width, units), BF16),) *...]
where the time goes in v3:
time: 55.1 us; the launch traced here: 54.9 us
  Pallas kernels  52.2 us (95%)
  local copies, waits for them, and re-layouts  2.03 us (4%)
  between operations  0.64 us (1%)
    pallas_call x1, Pallas kernels, kernel_body(): pl.pallas_call(functools.partial(exchange_kernel, experts, chunk), out_sh...  40.5 us
    pallas_call x1, Pallas kernels, kernel_body(): pl.pallas_call(weight_kernel, out_shape=(shape((width, units), BF16),) *...  11.8 us
    unnamed x1, local copies, waits for them, and re-layouts  2.03 us

profile of v3, /device:TPU:0, one launch (start us, length us, event | category | flops | bytes accessed | tf_op | source)
XLA Modules:
  0.0 54.9 jit_solution(15670652757698041927)
XLA Ops:
  0.6 40.5 %exchange.1 = (bf16[2880,128]{1,0:T(8,128)(2,1)}, bf16[64,1280]{1,0:T(8,128)(2,1)}, bf16[64,1280]{1,0:T(8,128)(2,1)}, bf16[64,1280]{1,0:T(8,128)(2,1)}, bf16[64,...) custom-call(bf16[2880,128]{1,0:T(8,128)(2,1)} %bitcast.14, bf16[2880,128]{1,0:T(8,128)(2,1)} %bitcast.15, s32[4,128]{1,0:T(4,128)} %bitcast.17, ...), custom_call_target="tpu_custom_call" | custom-call | tf_op jit(solution)/shard_map/exchange/pallas_call | solution.py:284
  41.1 11.8 %weight_grads.1 = (bf16[2880,1280]{1,0:T(8,128)(2,1)}, bf16[2880,1280]{1,0:T(8,128)(2,1)}, bf16[2880,1280]{1,0:T(8,128)(2,1)}) custom-call(bf16[64,1280]{1,0:T(8,128)(2,1)} %get-tuple-element.14.d_gate, bf16[64,1280]{1,0:T(8,128)(2,1)} %get-tuple-element.15.d_up, bf16[64,1280]{1,0:T(8,128)(2,1)} %get-tuple-element.16.act, ...), custom_call_target="tpu_custom_call" | custom-call | flops 1415577600 | bytes 22118400 | tf_op jit(solution)/shard_map/weight_grads/pallas_call | solution.py:330
  52.9 2.0 %copy.12 = bf16[128,2880]{0,1:T(8,128)(2,1)} copy(bf16[128,2880]{0,1:T(8,128)(2,1)} %bitcast.16) | data formatting | bytes 1474560

commit v4 on v3

--- a/solution.py
+++ b/solution.py
@@ -33,9 +33,9 @@
 def exchange_kernel(
     experts, chunk,
     tok, cot, ids, route, gate_hbm, up_hbm, down_hbm,
-    grad_tok, d_gate_out, d_up_out, act_out, x_out, c_out,
+    ret_in, place_out, d_gate_out, d_up_out, act_out, x_out, c_out,
     gate_w, up_w, down_w, send_x, send_c, recv_x, recv_c, stage,
-    gate_pre, up_pre, total, half_out, half_in, ret_out, ret_in,
+    gate_pre, up_pre, total, half_out, half_in, ret_out,
     w_sem, xs_sem, xr_sem, cs_sem, cr_sem, xfs_sem, xfr_sem, cfs_sem, cfr_sem,
     half_sem, rs_sem, rr_sem,
 ):
@@ -61,7 +61,7 @@
     def weight_copy(which, c):
         src = (gate_hbm, up_hbm, down_hbm)[which]
         dst = (gate_w, up_w, down_w)[which]
-        rows = pl.ds(pl.multiple_of(c * chunk, chunk), chunk)
+        rows = pl.ds(c * chunk if isinstance(c, int) else pl.multiple_of(c * chunk, chunk), chunk)
         return pltpu.make_async_copy(src.at[:, rows], dst.at[:, rows], w_sem.at[which, c])
 
     for which in range(3):
@@ -81,6 +81,7 @@
     earlier = jnp.where(iota((n_tok, n_tok), 0) < iota((n_tok, n_tok), 1), 1.0, 0.0)
     position = dot(member.astype(BF16), earlier.astype(BF16))
     place = jnp.where(position == line_slot, member, 0.0)
+    place_out[...] = place.astype(BF16)
     slot_weight = jnp.sum(place * weight, axis=1, keepdims=True)
     picks = [jnp.where(line_fold == j, place, 0.0).astype(BF16) for j in range(FOLD)]
 
@@ -165,29 +166,35 @@
             select = jnp.where(line_of == base + j * CAP, 1.0, 0.0).astype(BF16)
             out[:, lo:hi] = dot(select, recv[:, : hi - lo]).astype(BF16)
 
-    def gather(send, recv, sems, f_sems, out):
-        for d in near_last[::-1]:
+    def relay(send, recv, sems, f_sems, steps):
+        for d in steps:
             row_arrival(send, recv, *sems, d).wait_recv()
             forward(recv, *f_sems, d).start()
+
+    def finish(recv, f_sems, out):
         for d in range(experts):
             forward_arrival(recv, *f_sems, d).wait_recv()
         unpack(recv, out)
 
-    gather(send_x, recv_x, x_sems, xf_sems, x_out)
+    arrivals = near_last[::-1]
+    relay(send_x, recv_x, x_sems, xf_sems, arrivals)
+    finish(recv_x, xf_sems, x_out)
 
     def span(c):
-        return pl.ds(pl.multiple_of(c * chunk, chunk), chunk)
-
-    def project(c, carry):
+        return pl.ds(c * chunk if isinstance(c, int) else pl.multiple_of(c * chunk, chunk), chunk)
+
+    def project(c):
         weight_copy(0, c).wait()
         weight_copy(1, c).wait()
         x = x_out[...]
         gate_pre[:, span(c)] = dot(x, gate_w[:, span(c)])
         up_pre[:, span(c)] = dot(x, up_w[:, span(c)])
-        return carry
-
-    lax.fori_loop(0, chunks, project, 0)
-    gather(send_c, recv_c, c_sems, cf_sems, c_out)
+
+    share = -(-len(arrivals) // chunks)
+    for c in range(chunks):
+        project(c)
+        relay(send_c, recv_c, c_sems, cf_sems, arrivals[c * share : (c + 1) * share])
+    finish(recv_c, cf_sems, c_out)
 
     total[...] = jnp.zeros_like(total)
 
@@ -251,15 +258,16 @@
         forward(recv_c, *cf_sems, d).wait_send()
     for d in range(1, experts):
         ret_copy(d, False).wait_recv()
-    for j, (lo, hi) in enumerate(cols):
-        grad_tok[lo:hi, :] = lax.dot_general(
-            ret_in[:, : hi - lo], picks[j], FIRST, preferred_element_type=F32
-        ).astype(BF16)
     for d in range(1, experts):
         ret_copy(d, True).wait_send()
 
 
-def weight_kernel(d_gate, d_up, act, x, c, g_gate, g_up, g_down):
+def weight_kernel(per_fold, d_gate, d_up, act, x, c, ret, place, g_tok, g_gate, g_up, g_down):
+    fold = pl.program_id(0) // per_fold
+    line_fold = (iota(place.shape, 0) // CAP) % FOLD
+    take = jnp.where(line_fold == fold, place[...].astype(F32), 0.0).astype(BF16)
+    g_tok[...] = lax.dot_general(ret[...], take, FIRST, preferred_element_type=F32).astype(BF16)
+
     def term(a, b):
         return lax.dot_general(a[...], b[...], FIRST, preferred_element_type=F32).astype(BF16)
 
@@ -281,10 +289,11 @@
     hbm = pl.BlockSpec(memory_space=pl.ANY)
     sem = pltpu.SemaphoreType.DMA
     shape = jax.ShapeDtypeStruct
-    grad_tokens, d_gate, d_up, act, x, c = pl.pallas_call(
+    ret, place, d_gate, d_up, act, x, c = pl.pallas_call(
         functools.partial(exchange_kernel, experts, chunk),
         out_shape=(
-            shape((width, n_tok), BF16),
+            shape((lines, fold_width), BF16),
+            shape((lines, n_tok), BF16),
             shape((rows, units), BF16),
             shape((rows, units), BF16),
             shape((rows, units), BF16),
@@ -292,7 +301,7 @@
             shape((rows, width), BF16),
         ),
         in_specs=[vmem] * 4 + [hbm] * 3,
-        out_specs=(vmem,) * 6,
+        out_specs=(vmem,) * 7,
         scratch_shapes=[
             pltpu.VMEM((width, units), BF16),
             pltpu.VMEM((width, units), BF16),
@@ -308,7 +317,6 @@
             pltpu.VMEM((rows // 2, width), BF16),
             pltpu.VMEM((rows // 2, width), BF16),
             pltpu.VMEM((lines, fold_width), BF16),
-            pltpu.VMEM((lines, fold_width), BF16),
             sem((3, units // chunk)),
             sem((experts,)), sem((experts,)), sem((experts,)), sem((experts,)),
             sem((experts,)), sem((experts,)), sem((experts,)), sem((experts,)),
@@ -323,23 +331,28 @@
         gate_weight.T, up_weight.T, down_weight.T,
     )
 
-    step = 384
+    step = fold_width // 2 if fold_width % 256 == 0 else fold_width
+    per_fold = fold_width // step
     part = pl.BlockSpec((rows, step), lambda i: (0, i))
     whole = pl.BlockSpec((rows, units), lambda i: (0, 0))
     result = pl.BlockSpec((step, units), lambda i: (i, 0))
     grads = pl.pallas_call(
-        weight_kernel,
-        out_shape=(shape((width, units), BF16),) * 3,
+        functools.partial(weight_kernel, per_fold),
+        out_shape=(shape((width, n_tok), BF16),) + (shape((width, units), BF16),) * 3,
         grid=(pl.cdiv(width, step),),
-        in_specs=[whole, whole, whole, part, part],
-        out_specs=(result,) * 3,
+        in_specs=[
+            whole, whole, whole, part, part,
+            pl.BlockSpec((lines, step), lambda i: (0, i % per_fold)),
+            pl.BlockSpec((lines, n_tok), lambda i: (0, 0)),
+        ],
+        out_specs=(pl.BlockSpec((step, n_tok), lambda i: (i, 0)),) + (result,) * 3,
         compiler_params=pltpu.CompilerParams(vmem_limit_bytes=56 * 1024 * 1024),
         cost_estimate=pl.CostEstimate(
             flops=6 * rows * units * width, bytes_accessed=6 * units * width, transcendentals=0
         ),
         name="weight_grads",
-    )(d_gate, d_up, act, x, c)
-    return (grad_tokens.T, *(g.T for g in grads))
+    )(d_gate, d_up, act, x, c, ret, place)
+    return tuple(g.T for g in grads)
 
 
 def expert_backward(rows_x, rows_c, w_gate, w_up, w_down):

time: 55.1 us -> 52.2 us (0.947)
  local copies, waits for them, and re-layouts: 2.03 us -> 0 us
  Pallas kernels: 52.2 us -> 51.3 us
    unnamed x1 -> x0, local copies, waits for them, and re-layouts: 2.03 us -> none
    pallas_call x1, Pallas kernels: 40.5 us -> 39 us  [kernel_body(): pl.pallas_call(functools.partial(exchange_kernel, experts, chunk), out_sh...]
where the time goes in v4:
time: 52.2 us; the launch traced here: 51.9 us
  Pallas kernels  51.3 us (98%)
  between operations  0.64 us (1%)
    pallas_call x1, Pallas kernels, kernel_body(): pl.pallas_call(functools.partial(exchange_kernel, experts, chunk), out_sh...  39 us
    pallas_call x1, Pallas kernels, kernel_body(): pl.pallas_call(functools.partial(weight_kernel, per_fold), out_shape=(sha...  12.2 us

profile of v4, /device:TPU:0, one launch (start us, length us, event | category | flops | bytes accessed | tf_op | source)
XLA Modules:
  0.0 51.9 jit_solution(5991653311776695708)
XLA Ops:
  0.6 39.0 %exchange.1 = (bf16[128,768]{1,0:T(8,128)(2,1)}, bf16[128,128]{1,0:T(8,128)(2,1)}, bf16[64,1280]{1,0:T(8,128)(2,1)}, bf16[64,1280]{1,0:T(8,128)(2,1)}, bf16[64,1...) custom-call(bf16[2880,128]{1,0:T(8,128)(2,1)} %bitcast.14, bf16[2880,128]{1,0:T(8,128)(2,1)} %bitcast.15, ...), custom_call_target="tpu_custom_call" | custom-call | tf_op jit(solution)/shard_map/exchange/pallas_call | solution.py:292
  39.7 12.2 %weight_grads.1 = (bf16[2880,128]{1,0:T(8,128)(2,1)}, bf16[2880,1280]{1,0:T(8,128)(2,1)}, bf16[2880,1280]{1,0:T(8,128)(2,1)}, bf16[2880,1280]{1,0:T(8,128)(2,1)}) custom-call(bf16[64,1280]{1,0:T(8,128)(2,1)} %get-tuple-element.15.d_gate, bf16[64,1280]{1,0:T(8,128)(2,1)} %get-tuple-element.16.d_up, bf16[64,1280]{1,0:T(8,128)(2,1)} %get-tuple-element.17.act, ...), custom_call_target="tpu_custom_call" | custom-call | flops 1415577600 | bytes 22118400 | tf_op jit(solution)/shard_map/weight_grads/pallas_call | solution.py:339
